TPU v7x, 512 devices: a whole 4x8x8 slice. The times are simulated.
512 devices in a mesh: ex: 16 (over y_lo, x, core), lay: 32 (over y_hi, z).
Axes of the slice: x: 4, y: 8 (y_hi: 4, y_lo: 2; y = y_hi * 2 + y_lo), z: 8, core: 2. Of those that a mesh axis runs over, the one named last changes fastest.
Arguments:
- query_grads: bfloat16 [512, 32, 4096], P('ex', 'lay'), may hold values from -6 to 6
- store: bfloat16 [8192, 32, 4096], P('ex', 'lay'), may hold values from -6 to 6
- left_inv: float32 [32, 64, 64], P('lay'), may hold values from -0.75 to 0.75
- right_inv: float32 [32, 64, 64], P('lay'), may hold values from -0.75 to 0.75
- query_ids: int32 [512], replicated, may hold values from 0 to 16383
- block_offsets: int32 [16], P('ex'), may hold values from 0 to 15872, as said below
Outputs:
- scores: float32 [512, 8192], P('lay', 'ex')
Inputs may be any that keep to these rules, and one draw needn't show every extreme that they name: block_offsets[k] lies between 2 k * 512 and (2 k + 1) * 512, so the shards' ids never intersect.
All inputs are finite; a program needn't handle non-finite values.
Results may differ from a plain program's by a relative error of at most 0.0029.
Values may be sent and summed in bfloat16 or wider, within the bound.
A program may use at most 64 MiB of HBM per device.

v0:
```python
import jax
import jax.numpy as jnp
from jax import lax
from jax.sharding import PartitionSpec as P


def condition(grads, left_inv, right_inv):
    count, layers, entries = grads.shape
    side = left_inv.shape[1]
    mats = grads.astype(jnp.float32).reshape(count, layers, side, side)
    out = jnp.einsum(
        "lab,nlbc,lcd->nlad", left_inv, mats, right_inv, precision=lax.Precision.HIGHEST
    )
    return out.reshape(count, layers, entries).astype(jnp.bfloat16)


def per_device(query_grads, store, left_inv, right_inv, query_ids, block_offsets):
    gathered = lax.all_gather(query_grads, "ex", axis=0, tiled=True)
    conditioned = condition(gathered, left_inv, right_inv)
    total_q = conditioned.shape[0]
    local_ex = store.shape[0]
    width = store.shape[1] * store.shape[2]
    flat_q = conditioned.reshape(total_q, width)
    flat_s = store.reshape(local_ex, width)
    partial_value = lax.dot_general(
        flat_q, flat_s, (((1,), (1,)), ((), ())), preferred_element_type=jnp.float32
    )
    cond32 = flat_q.astype(jnp.float32)
    query_sq = jnp.sum(cond32 * cond32, axis=1)
    store32 = flat_s.astype(jnp.float32)
    example_sq = lax.psum(jnp.sum(store32 * store32, axis=1), "lay")
    my_rows = total_q // lax.axis_size("lay")
    first_row = lax.axis_index("lay") * my_rows
    summed = lax.psum_scatter(partial_value, "lay", scatter_dimension=0, tiled=True)
    every_query_sq = lax.psum(query_sq, "lay")
    my_query_sq = lax.dynamic_slice_in_dim(every_query_sq, first_row, my_rows, 0)
    scale = jnp.sqrt(jnp.float32(width * lax.axis_size("lay")))
    cosine = (
        summed
        * lax.rsqrt(my_query_sq + 1e-06)[:, None]
        * lax.rsqrt(example_sq + 1e-06)[None, :]
        * scale
    )
    my_ids = lax.dynamic_slice_in_dim(query_ids, first_row, my_rows, 0)
    example_ids = block_offsets[0] + jnp.arange(local_ex, dtype=jnp.int32)
    return jnp.where(my_ids[:, None] == example_ids[None, :], jnp.float32(0.0), cosine)


def solution(mesh):
    return jax.shard_map(
        per_device,
        mesh=mesh,
        in_specs=(
            P("ex", "lay", None),
            P("ex", "lay", None),
            P("lay", None, None),
            P("lay", None, None),
            P(),
            P("ex"),
        ),
        out_specs=P("lay", "ex"),
        check_vma=False,
    )
```

profile of v0, /device:TPU:2, one launch (start us, length us, event | category | flops | bytes accessed | tf_op | source)
XLA Modules:
  0.0 320.8 jit_solution(317802592910957439)
XLA Ops:
  6.5 0.0 copy-start
  6.5 0.0 all-gather.2.cloned.1.call-start
  6.5 0.7 all-gather.2.cloned.1.call-update
  7.3 0.0 copy-start.2
  7.3 0.0 reduce-scatter.2.cloned.1.call-start
  7.3 49.3 %all-gather.2.cloned.1.call-done = bf16[512,1,4096]{2,0,1:T(8,128)(2,1)} async-done(((bf16[32,1,4096]{2,0,1:T(8,128)(2,1)}), bf16[512,1,4096]{2,0,1:T(8,128)(2,1)}) %all-gather.2.cloned.1.call-update) | async-done | bytes 4194320 | tf_op jit(solution)/shard_map/all_gather | solution.py:18
  56.7 6.5 %copy.10 = bf16[512,1,4096]{0,2,1:T(8,128)(2,1)} copy(bf16[512,1,4096]{2,0,1:T(8,128)(2,1)} %all-gather.2.cloned.1.call-done) | data formatting | bytes 8388608 | tf_op jit(solution)/shard_map/all_gather | solution.py:18
  63.2 0.0 copy-done.2
  63.2 8.6 %fusion.4 = f32[512,64,64]{0,2,1:T(8,128)S(1)} fusion(bf16[512,64,64]{0,2,1:T(8,128)(2,1)} %bitcast.20, f32[1,64,64]{2,1,0:T(8,128)S(1)} %copy-done.2), kind=kOutput, calls=%fused_computation.6 | convolution fusion | flops 1610612736 | bytes 12599296 | tf_op jit(solution)/shard_map/lab,nlbc,lcd->nlad/dot_general | solution.py:11
  71.8 0.0 copy-done
  71.8 0.0 copy-start.1
  71.9 11.9 %multiply_reduce_fusion.1 = (f32[512]{0:T(512)S(1)}, bf16[512,64,64]{0,2,1:T(8,128)(2,1)S(1)}) fusion(f32[1,64,64]{2,1,0:T(8,128)S(1)} %copy-done, f32[512,64,64]{0,2,1:T(8,128)S(1)} %fusion.4), kind=kOutput, calls=%fused_computation.3 | convolution fusion | flops 1619000832 | bytes 12601344 | tf_op jit(solution)/shard_map/lab,nlbc,lcd->nlad/dot_general | solution.py:11
  83.7 0.0 copy-done.1
  83.7 3.4 %fusion.2 = f32[512,512]{1,0:T(8,128)} fusion(bf16[512,4096]{0,1:T(8,128)(2,1)S(1)} %bitcast.21, bf16[512,1,4096]{2,0,1:T(8,128)(2,1)S(1)} %copy-done.1), kind=kOutput, calls=%fused_computation.4 | convolution fusion | flops 2147483648 | bytes 9437184 | tf_op jit(solution)/shard_map/dot_general | solution.py:25
  87.1 0.0 reduce-scatter.2.cloned.1.call-update
  87.8 0.8 dynamic_slice.6
  88.5 3.1 multiply_reduce_fusion
  91.6 83.5 %all-reduce = (f32[512]{0:T(512)S(1)}, f32[512]{0:T(512)S(1)}) all-reduce(f32[512]{0:T(512)S(1)} %multiply_reduce_fusion, f32[512]{0:T(512)S(1)} %get-tuple-element.7), channel_id=1, replica_groups=mesh['ex'=16,'lay'=32] {'lay'}, use_global_device_ids=true, to_apply=%region_4.0 | all-reduce | flops 1024 | bytes 8192 | tf_op jit(solution)/shard_map/psum | solution.py:31
  175.1 0.1 add_rsqrt_fusion.1
  175.2 137.4 %reduce-scatter.2.cloned.1.call-done = f32[16,512]{1,0:T(8,128)} async-done(((f32[512,512]{1,0:T(8,128)}), f32[16,512]{1,0:T(8,128)}) %reduce-scatter.2.cloned.1.call-update) | async-done | bytes 32784 | tf_op jit(solution)/shard_map/reduce_scatter | solution.py:34
  312.5 1.4 multiply_select_fusion
  (2 shorter events, 0.0 us)
Async XLA Ops:
  6.5 65.3 %copy-start = (f32[1,64,64]{2,1,0:T(8,128)S(1)}, f32[1,64,64]{2,1,0:T(8,128)}, u32[]{:S(2)}) copy-start(f32[1,64,64]{2,1,0:T(8,128)} %param.9) | copy-start | bytes 49156
  6.5 50.1 %all-gather.2.cloned.1.call-start = ((), (), s32[]{:S(2)}) async-start(), calls=%async_computation.1 | async-start | bytes 4456448 | tf_op jit(solution)/shard_map/all_gather | solution.py:18
  7.3 55.9 %copy-start.2 = (f32[1,64,64]{2,1,0:T(8,128)S(1)}, f32[1,64,64]{2,1,0:T(8,128)}, u32[]{:S(2)}) copy-start(f32[1,64,64]{2,1,0:T(8,128)} %param.8) | copy-start | bytes 49156
  7.3 305.3 %reduce-scatter.2.cloned.1.call-start = ((), (), s32[]{:S(2)}) async-start(), calls=%async_computation.2 | async-start | bytes 1081344 | tf_op jit(solution)/shard_map/reduce_scatter | solution.py:34
  71.8 11.9 %copy-start.1 = (bf16[512,1,4096]{2,0,1:T(8,128)(2,1)S(1)}, bf16[512,1,4096]{2,0,1:T(8,128)(2,1)}, u32[]{:S(2)}) copy-start(bf16[512,1,4096]{2,0,1:T(8,128)(2,1)} %param.7) | copy-start | bytes 12582916
Sparse Core Ops, SparseCore 0:
  9.5 47.1 all-gather.1
  87.2 225.2 reduce-scatter.1
where the time goes:
time: 321 us
  waiting for transfers between devices  187 us (58%)
  blocking collectives  83.5 us (26%)
  matrix products  23.9 us (7%)
  between operations  14.1 us (4%)
  local copies, waits for them, and re-layouts  7.32 us (2%)
  other arithmetic  4.61 us (1%)
    reduce_scatter x1, waiting for transfers between devices, per_device(): lax.psum_scatter(partial_value, 'lay', scatter_dimension=0, tiled=True)  137 us
    psum x1, blocking collectives, per_device(): example_sq = lax.psum(jnp.sum(store32 * store32, axis=1), 'lay')  83.5 us
    all_gather x1, waiting for transfers between devices, per_device(): gathered = lax.all_gather(query_grads, 'ex', axis=0, tiled=True)  49.3 us
    dot_general x2, matrix products, condition(): jnp.einsum('lab,nlbc,lcd->nlad', left_inv, mats, right_inv, precision=lax...  20.5 us
    all_gather x1, local copies, waits for them, and re-layouts, per_device(): gathered = lax.all_gather(query_grads, 'ex', axis=0, tiled=True)  6.54 us
  transfers between devices with their start and end apart: 2, of which 2 were waited for; matrix products, arithmetic and copies ran while one was open for 1% of the time, Pallas kernels for 0%

commit v1 on v0

v1 whole, which is shorter than its diff:
```python
import functools

import jax
import jax.numpy as jnp
from jax import lax
from jax.experimental import pallas as pl
from jax.experimental.pallas import tpu as pltpu
from jax.sharding import PartitionSpec as P

F32, BF16 = jnp.float32, jnp.bfloat16
MESH = pl.DeviceIdType.MESH
NT = (((1,), (1,)), ((), ()))
NN = (((1,), (0,)), ((), ()))

CHIPS = [(0, 0), (0, 1), (1, 0), (3, 0), (2, 0), (1, 1), (3, 1), (2, 1)]
BATCHES = [(0, 1), (1, 4), (4, 7), (7, 8)]
UNIT = 16
SIDE = 64


def slot(dx, dy):
    return CHIPS.index((dx % 4, dy % 2))


def unit(chip, other_core, half):
    return chip * 4 + other_core * 2 + half


def rows(u, n=1):
    return pl.ds(u * UNIT, n * UNIT)


def parts(value, n):
    out = []
    for _ in range(n):
        top = value.astype(BF16)
        out.append(top)
        value = value - top.astype(F32)
    return out


def dot(a, b, dims=NN):
    return lax.dot_general(a, b, dims, preferred_element_type=F32)


def condition(g_ref, left_ref, right_ref, mid_ref, out_ref, q_ref):
    count = g_ref.shape[0]
    pairs = SIDE // 2
    right = right_ref[...]
    wide = jnp.concatenate([right, right], axis=1)
    tall = jnp.concatenate([wide, wide], axis=0)
    row = lax.broadcasted_iota(jnp.int32, tall.shape, 0) < SIDE
    lane = lax.broadcasted_iota(jnp.int32, tall.shape, 1) < SIDE
    same = jnp.where(row == lane, tall, 0.0)
    cross = jnp.where(row == lane, 0.0, tall)
    both = jnp.concatenate([same, cross], axis=1)
    grads = jnp.concatenate([g_ref[:, p * 128 : (p + 1) * 128] for p in range(pairs)], axis=0)
    total = None
    for part in parts(both, 3):
        term = dot(grads, part)
        total = term if total is None else total + term
    mid_ref[0] = total[:, :128]
    mid_ref[1] = total[:, 128:]

    pick_r = lax.broadcasted_iota(jnp.int32, (SIDE, SIDE), 0)
    pick_c = lax.broadcasted_iota(jnp.int32, (SIDE, SIDE), 1)
    even_odd = jnp.where(pick_c < pairs, 2 * pick_c, 2 * (pick_c - pairs) + 1)
    odd_even = jnp.where(pick_c < pairs, 2 * pick_c + 1, 2 * (pick_c - pairs))
    to_eo = jnp.where(pick_r == even_odd, 1.0, 0.0).astype(BF16)
    to_oe = jnp.where(pick_r == odd_even, 1.0, 0.0).astype(BF16)
    out_ref[0:SIDE, 0:SIDE] = left_ref[...]
    even_rows = parts(out_ref[pl.ds(0, pairs, stride=2), :][:, :SIDE], 3)
    odd_rows = parts(out_ref[pl.ds(1, pairs, stride=2), :][:, :SIDE], 3)
    high, middle, low = [
        jnp.concatenate([dot(e, to_eo), dot(o, to_oe)], axis=0).astype(BF16)
        for e, o in zip(even_rows, odd_rows)
    ]
    left = jnp.concatenate([high, high, middle, middle, high, low], axis=1)

    lane2 = lax.broadcasted_iota(jnp.int32, (pairs, 256), 1) % 128 < SIDE
    for n in range(0, count, 2):
        columns = []
        for i in (n, n + 1):
            x = jnp.concatenate([mid_ref[t, pl.ds(i, pairs, stride=count), :] for t in range(2)], axis=0)
            xh, xm, xl = parts(x, 3)
            columns.append(jnp.concatenate([xh, xm, xh, xm, xl, xh], axis=0))
        res = dot(left, jnp.concatenate(columns, axis=1))
        res = jnp.where(lane2, res[:pairs], res[pairs:])
        out_ref[n * pairs : (n + 1) * pairs, :] = res[:, :128]
        out_ref[(n + 1) * pairs : (n + 2) * pairs, :] = res[:, 128:]

    squares = jnp.zeros((count, 128), F32)
    for p in range(pairs):
        value = out_ref[pl.ds(p, count, stride=pairs), :].astype(BF16)
        q_ref[0:count, p * 128 : (p + 1) * 128] = value
        wide_value = value.astype(F32)
        squares = squares + wide_value * wide_value
    return squares


def kernel(
    g_hbm, s_hbm, left_ref, right_ref, ids_ref, off_ref, out_ref,
    g_ref, s_ref, mid_ref, cond_ref, q_ref, p_ref, z_ref, ys_ref, yr_ref,
    nv_ref, nz_ref, ny_ref, nt_ref, nb_ref,
    load_sem, g_send, g_recv, z_send, z_recv, y_send, y_recv,
    nz_send, nz_recv, ny_send, ny_recv, nb_send, nb_recv,
):
    ex, lay = lax.axis_index("ex"), lax.axis_index("lay")
    core, x, yl = ex % 2, (ex // 2) % 4, ex // 8
    z, yh = lay % 8, lay // 8
    sibling = ex + 1 - 2 * core
    x_up = yl * 8 + ((x + 1) % 4) * 2 + core
    x_down = yl * 8 + ((x + 3) % 4) * 2 + core
    y_mate = (ex + 8) % 16

    barrier = pltpu.get_barrier_semaphore()
    for k in range(1, 16):
        pl.semaphore_signal(barrier, inc=1, device_id=((ex + k) % 16, lay), device_id_type=MESH)
    for k in range(1, 8):
        pl.semaphore_signal(barrier, inc=1, device_id=(ex, yh * 8 + (z + k) % 8), device_id_type=MESH)
    for k in range(1, 4):
        pl.semaphore_signal(barrier, inc=1, device_id=(ex, (lay + 8 * k) % 32), device_id_type=MESH)

    load_g = pltpu.make_async_copy(g_hbm, g_ref, load_sem.at[0])
    load_g.start()
    load_s = [
        pltpu.make_async_copy(s_hbm.at[pl.ds(128 * i, 128)], s_ref.at[pl.ds(128 * i, 128)], load_sem.at[1 + i])
        for i in range(4)
    ]
    for copy in load_s:
        copy.start()
    nv_ref[...] = jnp.zeros_like(nv_ref)
    load_g.wait()
    squares = condition(g_ref, left_ref, right_ref, mid_ref, cond_ref, q_ref)

    pl.semaphore_wait(barrier, 25)

    def send(src, dst, to):
        pltpu.make_async_remote_copy(
            src_ref=q_ref.at[rows(src)], dst_ref=q_ref.at[rows(dst)], send_sem=g_send.at[0],
            recv_sem=g_recv.at[dst], device_id=(to, lay), device_id_type=MESH,
        ).start()

    def arrived(u):
        pltpu.make_async_copy(q_ref.at[rows(u)], q_ref.at[rows(u)], g_recv.at[u]).wait()

    def up(dx, dy, half):
        send(unit(slot(dx, dy), 0, half), unit(slot(dx - 1, dy), 0, half), x_up)

    def down(dx, dy, half):
        send(unit(slot(dx, dy), 0, half), unit(slot(dx + 1, dy), 0, half), x_down)

    def across(dx, dy, half):
        send(unit(slot(dx, dy), 0, half), unit(slot(dx, dy + 1), 0, half), y_mate)

    def share(dx, dy, half):
        send(unit(slot(dx, dy), 0, half), unit(slot(dx, dy), 1, half), sibling)

    def take(dx, dy, half):
        arrived(unit(slot(dx, dy), 0, half))

    across(0, 0, 0)
    up(0, 0, 0)
    down(0, 0, 0)
    share(0, 0, 0)
    across(0, 0, 1)
    up(0, 0, 1)
    down(0, 0, 1)
    share(0, 0, 1)

    for copy in load_s:
        copy.wait()
    nv_ref[4:5, 0:32] = jnp.sum(squares.T, axis=0, keepdims=True)

    for block in range(4):
        pieces = []
        for part in range(2):
            total = jnp.zeros((64, 128), F32)
            for t in range(32):
                value = s_ref[block * 128 + part * 64 : block * 128 + part * 64 + 64, t * 128 : (t + 1) * 128].astype(F32)
                total = total + value * value
            pieces.append(total)
        nv_ref[block : block + 1, :] = jnp.sum(jnp.concatenate(pieces, axis=0).T, axis=0, keepdims=True)

    def z_norm(k):
        return pltpu.make_async_remote_copy(
            src_ref=nv_ref, dst_ref=nz_ref.at[k], send_sem=nz_send.at[k], recv_sem=nz_recv.at[k],
            device_id=(ex, yh * 8 + (z + k + 1) % 8), device_id_type=MESH,
        )

    for k in range(7):
        z_norm(k).start()

    def y_norm(k):
        return pltpu.make_async_remote_copy(
            src_ref=ny_ref.at[3], dst_ref=ny_ref.at[k], send_sem=ny_send.at[k], recv_sem=ny_recv.at[k],
            device_id=(ex, (lay + 8 * (k + 1)) % 32), device_id_type=MESH,
        )

    def b_norm(k):
        return pltpu.make_async_remote_copy(
            src_ref=nt_ref, dst_ref=nb_ref, send_sem=nb_send.at[k], recv_sem=nb_recv.at[0],
            device_id=((ex + k + 1) % 16, lay), device_id_type=MESH,
        )

    owner = lay // 2

    def norms_over_z():
        total = nv_ref[...]
        for k in range(7):
            z_norm(k).wait_recv()
            total = total + nz_ref[k]
        ny_ref[3] = total
        for k in range(3):
            y_norm(k).start()

    def norms_over_y():
        total = ny_ref[3]
        for k in range(3):
            y_norm(k).wait_recv()
            total = total + ny_ref[k]
        nt_ref[...] = total

        @pl.when(ex == owner)
        def _():
            for k in range(15):
                b_norm(k).start()

    def place(chip):
        dx, dy = CHIPS[chip]
        return (x + dx) % 4, (yl + dy) % 2

    def multiply(batch):
        first, last = BATCHES[batch]
        span = rows(first * 4, 4 * (last - first))
        p_ref[span, :] = dot(q_ref[span, :], s_ref[...], NT).astype(BF16)
        for chip in range(first, last):
            its_x, _ = place(chip)
            for other in range(2):
                for half in range(2):
                    u = unit(chip, other, half)
                    its_core = (core + other) % 2
                    goal = 4 * (its_x % 2) + 2 * its_core + half

                    @pl.when(goal != z)
                    def _():
                        pltpu.make_async_remote_copy(
                            src_ref=p_ref.at[rows(u)], dst_ref=z_ref.at[chip, (z + 8 - goal) % 8],
                            send_sem=z_send.at[chip], recv_sem=z_recv.at[chip],
                            device_id=(ex, yh * 8 + goal), device_id_type=MESH,
                        ).start()

    def mine(chip):
        its_x, _ = place(chip)
        return its_x % 2 == z // 4

    def goal_of(chip):
        its_x, its_y = place(chip)
        return 2 * its_y + its_x // 2

    def y_copy(chip):
        goal = goal_of(chip)
        return pltpu.make_async_remote_copy(
            src_ref=ys_ref.at[chip], dst_ref=yr_ref.at[(yh + 4 - goal) % 4],
            send_sem=y_send.at[chip], recv_sem=y_recv.at[(yh + 4 - goal) % 4],
            device_id=(ex, goal * 8 + z), device_id_type=MESH,
        )

    def sum_over_z(batch):
        first, last = BATCHES[batch]
        for chip in range(first, last):

            @pl.when(mine(chip))
            def _():
                pltpu.make_async_copy(
                    z_ref.at[chip, pl.ds(1, 7)], z_ref.at[chip, pl.ds(1, 7)], z_recv.at[chip]
                ).wait()
                within = (((z % 4) // 2 + core) % 2) * 2 + z % 2
                start = pl.multiple_of((chip * 4 + within) * UNIT, UNIT)
                total = p_ref[pl.ds(start, UNIT), :].astype(F32)
                for k in range(1, 8):
                    total = total + z_ref[chip, k].astype(F32)
                goal = goal_of(chip)

                @pl.when(goal == yh)
                def _():
                    yr_ref[0] = total

                @pl.when(goal != yh)
                def _():
                    ys_ref[chip] = total
                    y_copy(chip).start()

    arrived(unit(0, 1, 0))
    arrived(unit(0, 1, 1))
    multiply(0)

    take(0, 1, 0)
    up(0, 1, 0)
    down(0, 1, 0)
    share(0, 1, 0)
    take(3, 0, 0)
    up(3, 0, 0)
    share(3, 0, 0)
    take(1, 0, 0)
    share(1, 0, 0)
    norms_over_z()
    take(1, 0, 1)
    down(1, 0, 1)
    across(1, 0, 1)
    share(1, 0, 1)
    take(3, 0, 1)
    across(3, 0, 1)
    share(3, 0, 1)
    take(0, 1, 1)
    share(0, 1, 1)
    for chip in range(*BATCHES[1]):
        arrived(unit(chip, 1, 0))
        arrived(unit(chip, 1, 1))
    multiply(1)
    sum_over_z(0)

    take(2, 0, 0)
    share(2, 0, 0)
    take(2, 0, 1)
    across(2, 0, 1)
    share(2, 0, 1)
    take(3, 1, 0)

    @pl.when(core == 0)
    def _():
        up(3, 1, 0)

    share(3, 1, 0)
    take(1, 1, 0)

    @pl.when(core == 1)
    def _():
        down(1, 1, 0)

    share(1, 1, 0)
    norms_over_y()
    take(1, 1, 1)
    share(1, 1, 1)
    take(3, 1, 1)
    share(3, 1, 1)
    for chip in range(*BATCHES[2]):
        arrived(unit(chip, 1, 0))
        arrived(unit(chip, 1, 1))
    multiply(2)
    sum_over_z(1)

    take(2, 1, 0)
    share(2, 1, 0)
    take(2, 1, 1)
    share(2, 1, 1)
    arrived(unit(7, 1, 0))
    arrived(unit(7, 1, 1))
    multiply(3)
    sum_over_z(2)

    @pl.when(ex == owner)
    def _():
        nb_ref[...] = nt_ref[...]

    @pl.when(ex != owner)
    def _():
        b_norm(0).wait_recv()

    pltpu.make_async_copy(q_ref.at[rows(0, 30)], q_ref.at[rows(0, 30)], g_send.at[0]).wait()
    for k in range(7):
        z_norm(k).wait_send()
    for k in range(3):
        y_norm(k).wait_send()

    @pl.when(ex == owner)
    def _():
        for k in range(15):
            b_norm(k).wait_send()

    sum_over_z(3)
    for chip in range(8):

        @pl.when(mine(chip))
        def _():
            pltpu.make_async_copy(p_ref.at[rows(0, 3)], p_ref.at[rows(0, 3)], z_send.at[chip]).wait()

        @pl.when(jnp.logical_not(mine(chip)))
        def _():
            pltpu.make_async_copy(p_ref.at[rows(0, 4)], p_ref.at[rows(0, 4)], z_send.at[chip]).wait()

    columns = nb_ref[...].T[:, 4:5]
    query_sq = jnp.where(lay % 2 == 0, columns[:UNIT], columns[UNIT : 2 * UNIT])
    query_scale = lax.rsqrt(query_sq + 1e-06)
    scale = jnp.sqrt(F32(SIDE * SIDE * 32))
    which = lax.broadcasted_iota(jnp.int32, (UNIT, 128), 0)
    ids = jnp.zeros((UNIT, 128), jnp.int32)
    for i in range(UNIT):
        ids = jnp.where(which == i, ids_ref[lay * UNIT + i], ids)
    place_of = lax.broadcasted_iota(jnp.int32, (UNIT, 128), 1) + off_ref[0]
    for k in range(1, 4):
        pltpu.make_async_copy(yr_ref.at[k], yr_ref.at[k], y_recv.at[k]).wait()
    for block in range(4):
        span = slice(block * 128, (block + 1) * 128)
        total = yr_ref[0, :, span] + yr_ref[1, :, span] + yr_ref[2, :, span] + yr_ref[3, :, span]
        example_scale = lax.rsqrt(nt_ref[block : block + 1, :] + 1e-06)
        value = total * query_scale * example_scale * scale
        out_ref[:, span] = jnp.where(ids == place_of + block * 128, F32(0.0), value)
    for chip in range(8):

        @pl.when(jnp.logical_and(mine(chip), goal_of(chip) != yh))
        def _():
            y_copy(chip).wait_send()


def per_device(query_grads, store, left_inv, right_inv, query_ids, block_offsets):
    count, _, width = query_grads.shape
    examples = store.shape[0]
    vmem = pl.BlockSpec(memory_space=pltpu.VMEM)
    smem = pl.BlockSpec(memory_space=pltpu.SMEM)
    hbm = pl.BlockSpec(memory_space=pl.ANY)
    dma = pltpu.SemaphoreType.DMA
    return pl.pallas_call(
        kernel,
        out_shape=jax.ShapeDtypeStruct((UNIT, examples), F32),
        in_specs=[hbm, hbm, vmem, vmem, smem, smem],
        out_specs=vmem,
        scratch_shapes=[
            pltpu.VMEM((count, width), BF16),
            pltpu.VMEM((examples, width), BF16),
            pltpu.VMEM((2, 1024, 128), F32),
            pltpu.VMEM((1024, 128), F32),
            pltpu.VMEM((512, width), BF16),
            pltpu.VMEM((512, examples), BF16),
            pltpu.VMEM((8, 8, UNIT, examples), BF16),
            pltpu.VMEM((8, UNIT, examples), F32),
            pltpu.VMEM((4, UNIT, examples), F32),
            pltpu.VMEM((8, 128), F32),
            pltpu.VMEM((7, 8, 128), F32),
            pltpu.VMEM((4, 8, 128), F32),
            pltpu.VMEM((8, 128), F32),
            pltpu.VMEM((8, 128), F32),
            dma((5,)),
            dma((1,)),
            dma((32,)),
            dma((8,)),
            dma((8,)),
            dma((8,)),
            dma((4,)),
            dma((7,)),
            dma((7,)),
            dma((3,)),
            dma((3,)),
            dma((15,)),
            dma((1,)),
        ],
        compiler_params=pltpu.CompilerParams(
            collective_id=0, has_side_effects=True, vmem_limit_bytes=40 * 2**20
        ),
        cost_estimate=pl.CostEstimate(
            flops=2 * 512 * examples * width, bytes_accessed=(examples + count) * width * 2, transcendentals=0
        ),
    )(
        query_grads.reshape(count, width),
        store.reshape(examples, width),
        left_inv.reshape(SIDE, SIDE),
        right_inv.reshape(SIDE, SIDE),
        query_ids,
        block_offsets,
    )


def solution(mesh):
    return jax.shard_map(
        per_device,
        mesh=mesh,
        in_specs=(
            P("ex", "lay", None),
            P("ex", "lay", None),
            P("lay", None, None),
            P("lay", None, None),
            P(),
            P("ex"),
        ),
        out_specs=P("lay", "ex"),
        check_vma=False,
    )
```

time: 321 us -> 54.4 us (0.17)
  the two profiles are of different devices: /device:TPU:2 before, /device:TPU:24 now
where the time goes in v1:
time: 54.4 us; the launch traced here: 54.1 us
  Pallas kernels  47.4 us (87%)
  local copies, waits for them, and re-layouts  5.94 us (11%)
  between operations  0.67 us (1%)
    pallas_call x1, Pallas kernels, per_device(): pl.pallas_call(kernel, out_shape=jax.ShapeDtypeStruct((UNIT, examples), F...  47.4 us
    unnamed x11, local copies, waits for them, and re-layouts  5.94 us

profile of v1, /device:TPU:24, one launch (start us, length us, event | category | flops | bytes accessed | tf_op | source)
XLA Modules:
  0.0 54.1 jit_solution(2861388439423755649)
XLA Ops:
  0.7 0.0 copy-start
  0.7 2.2 %copy-done = bf16[512,1,4096]{2,0,1:T(8,128)(2,1)S(1)} copy-done((bf16[512,1,4096]{2,0,1:T(8,128)(2,1)S(1)}, bf16[512,1,4096]{2,0,1:T(8,128)(2,1)}, u32[]{:S(2)}) %copy-start) | copy-done | bytes 4194328
  2.8 0.0 copy-start.1
  2.8 0.9 %copy-done.1 = bf16[32,1,4096]{2,0,1:T(8,128)(2,1)S(1)} copy-done((bf16[32,1,4096]{2,0,1:T(8,128)(2,1)S(1)}, bf16[32,1,4096]{2,0,1:T(8,128)(2,1)}, u32[]{:S(2)}) %copy-start.1) | copy-done | bytes 262168
  3.8 0.0 copy-start.2
  3.8 0.8 %copy-done.2 = f32[1,64,64]{2,1,0:T(8,128)S(1)} copy-done((f32[1,64,64]{2,1,0:T(8,128)S(1)}, f32[1,64,64]{2,1,0:T(8,128)}, u32[]{:S(2)}) %copy-start.2) | copy-done | bytes 16408
  4.5 0.0 copy-start.3
  4.6 0.8 %copy-done.3 = f32[1,64,64]{2,1,0:T(8,128)S(1)} copy-done((f32[1,64,64]{2,1,0:T(8,128)S(1)}, f32[1,64,64]{2,1,0:T(8,128)}, u32[]{:S(2)}) %copy-start.3) | copy-done | bytes 16408
  5.3 0.0 copy-start.4
  5.3 0.7 %copy-done.4 = s32[512]{0:T(512)S(1)} copy-done((s32[512]{0:T(512)S(1)}, s32[512]{0:T(512)}, u32[]{:S(2)}) %copy-start.4) | copy-done | bytes 2072
  6.0 47.4 %shard_map.64 = f32[16,512]{1,0:T(8,128)S(1)} custom-call(bf16[32,4096]{1,0:T(8,128)(2,1)S(1)} %bitcast.5, bf16[512,4096]{1,0:T(8,128)(2,1)S(1)} %bitcast.4, f32[64,64]{1,0:T(8,128)S(1)} %bitcast.6, f32[64,64]{1,0:T(8,128)S(1)} %bitcast.7, s32[512]{0:T(512)S(1)} %copy-done.4, s32[1]{0:T(128)S(6)} %copy.8.off_ref), custom_call_target="tpu_custom_call" | custom-call | flops 2147483648 | bytes 4456448 | tf_op jit(solution)/shard_map/pallas_call | solution.py:423
  53.4 0.6 %copy.9 = f32[16,512]{1,0:T(8,128)} copy(f32[16,512]{1,0:T(8,128)S(1)} %shard_map.64) | data formatting | bytes 65536
Async XLA Ops:
  0.7 2.2 %copy-start = (bf16[512,1,4096]{2,0,1:T(8,128)(2,1)S(1)}, bf16[512,1,4096]{2,0,1:T(8,128)(2,1)}, u32[]{:S(2)}) copy-start(bf16[512,1,4096]{2,0,1:T(8,128)(2,1)} %param.7) | copy-start | bytes 12582916
  2.8 0.9 %copy-start.1 = (bf16[32,1,4096]{2,0,1:T(8,128)(2,1)S(1)}, bf16[32,1,4096]{2,0,1:T(8,128)(2,1)}, u32[]{:S(2)}) copy-start(bf16[32,1,4096]{2,0,1:T(8,128)(2,1)} %param.6) | copy-start | bytes 786436
  3.8 0.8 %copy-start.2 = (f32[1,64,64]{2,1,0:T(8,128)S(1)}, f32[1,64,64]{2,1,0:T(8,128)}, u32[]{:S(2)}) copy-start(f32[1,64,64]{2,1,0:T(8,128)} %param.8) | copy-start | bytes 49156
  4.5 0.8 %copy-start.3 = (f32[1,64,64]{2,1,0:T(8,128)S(1)}, f32[1,64,64]{2,1,0:T(8,128)}, u32[]{:S(2)}) copy-start(f32[1,64,64]{2,1,0:T(8,128)} %param.9) | copy-start | bytes 49156
  5.3 0.7 %copy-start.4 = (s32[512]{0:T(512)S(1)}, s32[512]{0:T(512)}, u32[]{:S(2)}) copy-start(s32[512]{0:T(512)} %ids_ref.1) | copy-start | bytes 6148

commit v2 on v1

--- a/solution.py
+++ b/solution.py
@@ -13,17 +13,23 @@
 NN = (((1,), (0,)), ((), ()))
 
 CHIPS = [(0, 0), (0, 1), (1, 0), (3, 0), (2, 0), (1, 1), (3, 1), (2, 1)]
-BATCHES = [(0, 1), (1, 4), (4, 7), (7, 8)]
+BATCHES = [
+    [(0, 0, 0), (0, 0, 1)],
+    [(1, 0, 1), (3, 0, 1), (0, 1, 1)],
+    [(1, 0, 0), (3, 0, 0), (0, 1, 0)],
+    [(2, 0, 1), (1, 1, 0), (3, 1, 0)],
+    [(2, 0, 0), (1, 1, 1), (3, 1, 1)],
+    [(2, 1, 0), (2, 1, 1)],
+]
+PLACES = [
+    (dx, dy, other, half) for batch in BATCHES for other in range(2) for dx, dy, half in batch
+]
 UNIT = 16
 SIDE = 64
 
 
-def slot(dx, dy):
-    return CHIPS.index((dx % 4, dy % 2))
-
-
-def unit(chip, other_core, half):
-    return chip * 4 + other_core * 2 + half
+def unit(dx, dy, other, half):
+    return PLACES.index((dx % 4, dy % 2, other, half))
 
 
 def rows(u, n=1):
@@ -43,8 +49,7 @@
     return lax.dot_general(a, b, dims, preferred_element_type=F32)
 
 
-def condition(g_ref, left_ref, right_ref, mid_ref, out_ref, q_ref):
-    count = g_ref.shape[0]
+def factors(left_ref, right_ref, tmp_ref):
     pairs = SIDE // 2
     right = right_ref[...]
     wide = jnp.concatenate([right, right], axis=1)
@@ -53,14 +58,7 @@
     lane = lax.broadcasted_iota(jnp.int32, tall.shape, 1) < SIDE
     same = jnp.where(row == lane, tall, 0.0)
     cross = jnp.where(row == lane, 0.0, tall)
-    both = jnp.concatenate([same, cross], axis=1)
-    grads = jnp.concatenate([g_ref[:, p * 128 : (p + 1) * 128] for p in range(pairs)], axis=0)
-    total = None
-    for part in parts(both, 3):
-        term = dot(grads, part)
-        total = term if total is None else total + term
-    mid_ref[0] = total[:, :128]
-    mid_ref[1] = total[:, 128:]
+    right_parts = parts(jnp.concatenate([same, cross], axis=1), 3)
 
     pick_r = lax.broadcasted_iota(jnp.int32, (SIDE, SIDE), 0)
     pick_c = lax.broadcasted_iota(jnp.int32, (SIDE, SIDE), 1)
@@ -68,39 +66,50 @@
     odd_even = jnp.where(pick_c < pairs, 2 * pick_c + 1, 2 * (pick_c - pairs))
     to_eo = jnp.where(pick_r == even_odd, 1.0, 0.0).astype(BF16)
     to_oe = jnp.where(pick_r == odd_even, 1.0, 0.0).astype(BF16)
-    out_ref[0:SIDE, 0:SIDE] = left_ref[...]
-    even_rows = parts(out_ref[pl.ds(0, pairs, stride=2), :][:, :SIDE], 3)
-    odd_rows = parts(out_ref[pl.ds(1, pairs, stride=2), :][:, :SIDE], 3)
+    tmp_ref[0:SIDE, :] = jnp.concatenate([left_ref[...], jnp.zeros((SIDE, SIDE), F32)], axis=1)
+    even_rows = parts(tmp_ref[pl.ds(0, pairs, stride=2), :][:, :SIDE], 3)
+    odd_rows = parts(tmp_ref[pl.ds(1, pairs, stride=2), :][:, :SIDE], 3)
     high, middle, low = [
         jnp.concatenate([dot(e, to_eo), dot(o, to_oe)], axis=0).astype(BF16)
         for e, o in zip(even_rows, odd_rows)
     ]
     left = jnp.concatenate([high, high, middle, middle, high, low], axis=1)
-
-    lane2 = lax.broadcasted_iota(jnp.int32, (pairs, 256), 1) % 128 < SIDE
-    for n in range(0, count, 2):
+    return left, right_parts
+
+
+def condition(g_ref, half, left, right_parts, mid_ref, tmp_ref, q_ref):
+    pairs = SIDE // 2
+    mine = slice(half * UNIT, (half + 1) * UNIT)
+    grads = jnp.concatenate([g_ref[mine, p * 128 : (p + 1) * 128] for p in range(pairs)], axis=0)
+    total = None
+    for part in right_parts:
+        term = dot(grads, part)
+        total = term if total is None else total + term
+    mid_ref[0] = total[:, :128]
+    mid_ref[1] = total[:, 128:]
+    lane = lax.broadcasted_iota(jnp.int32, (pairs, 256), 1) % 128 < SIDE
+    for n in range(0, UNIT, 2):
         columns = []
         for i in (n, n + 1):
-            x = jnp.concatenate([mid_ref[t, pl.ds(i, pairs, stride=count), :] for t in range(2)], axis=0)
+            x = jnp.concatenate([mid_ref[t, pl.ds(i, pairs, stride=UNIT), :] for t in range(2)], axis=0)
             xh, xm, xl = parts(x, 3)
             columns.append(jnp.concatenate([xh, xm, xh, xm, xl, xh], axis=0))
         res = dot(left, jnp.concatenate(columns, axis=1))
-        res = jnp.where(lane2, res[:pairs], res[pairs:])
-        out_ref[n * pairs : (n + 1) * pairs, :] = res[:, :128]
-        out_ref[(n + 1) * pairs : (n + 2) * pairs, :] = res[:, 128:]
-
-    squares = jnp.zeros((count, 128), F32)
+        res = jnp.where(lane, res[:pairs], res[pairs:])
+        tmp_ref[n * pairs : (n + 1) * pairs, :] = res[:, :128]
+        tmp_ref[(n + 1) * pairs : (n + 2) * pairs, :] = res[:, 128:]
+    squares = jnp.zeros((UNIT, 128), F32)
     for p in range(pairs):
-        value = out_ref[pl.ds(p, count, stride=pairs), :].astype(BF16)
-        q_ref[0:count, p * 128 : (p + 1) * 128] = value
+        value = tmp_ref[pl.ds(p, UNIT, stride=pairs), :].astype(BF16)
+        q_ref[mine, p * 128 : (p + 1) * 128] = value
         wide_value = value.astype(F32)
         squares = squares + wide_value * wide_value
     return squares
 
 
 def kernel(
-    g_hbm, s_hbm, left_ref, right_ref, ids_ref, off_ref, out_ref,
-    g_ref, s_ref, mid_ref, cond_ref, q_ref, p_ref, z_ref, ys_ref, yr_ref,
+    g_hbm, s_hbm, left_hbm, right_hbm, ids_hbm, off_ref, out_ref,
+    g_ref, s_ref, left_ref, right_ref, ids_ref, mid_ref, cond_ref, q_ref, p_ref, z_ref, ys_ref, yr_ref,
     nv_ref, nz_ref, ny_ref, nt_ref, nb_ref,
     load_sem, g_send, g_recv, z_send, z_recv, y_send, y_recv,
     nz_send, nz_recv, ny_send, ny_recv, nb_send, nb_recv,
@@ -121,17 +130,24 @@
     for k in range(1, 4):
         pl.semaphore_signal(barrier, inc=1, device_id=(ex, (lay + 8 * k) % 32), device_id_type=MESH)
 
-    load_g = pltpu.make_async_copy(g_hbm, g_ref, load_sem.at[0])
-    load_g.start()
+    first = [
+        pltpu.make_async_copy(src, dst, load_sem.at[4 + i])
+        for i, (src, dst) in enumerate([(right_hbm, right_ref), (g_hbm, g_ref), (left_hbm, left_ref)])
+    ]
+    small = [pltpu.make_async_copy(ids_hbm, ids_ref, load_sem.at[7])]
+    for copy in first:
+        copy.start()
     load_s = [
-        pltpu.make_async_copy(s_hbm.at[pl.ds(128 * i, 128)], s_ref.at[pl.ds(128 * i, 128)], load_sem.at[1 + i])
+        pltpu.make_async_copy(s_hbm.at[pl.ds(128 * i, 128)], s_ref.at[pl.ds(128 * i, 128)], load_sem.at[i])
         for i in range(4)
     ]
-    for copy in load_s:
+    for copy in load_s + small:
         copy.start()
     nv_ref[...] = jnp.zeros_like(nv_ref)
-    load_g.wait()
-    squares = condition(g_ref, left_ref, right_ref, mid_ref, cond_ref, q_ref)
+    for copy in first:
+        copy.wait()
+    left, right_parts = factors(left_ref, right_ref, cond_ref.at[1])
+    squares_1 = condition(g_ref, 1, left, right_parts, mid_ref.at[1], cond_ref.at[1], q_ref)
 
     pl.semaphore_wait(barrier, 25)
 
@@ -145,30 +161,32 @@
         pltpu.make_async_copy(q_ref.at[rows(u)], q_ref.at[rows(u)], g_recv.at[u]).wait()
 
     def up(dx, dy, half):
-        send(unit(slot(dx, dy), 0, half), unit(slot(dx - 1, dy), 0, half), x_up)
+        send(unit(dx, dy, 0, half), unit(dx - 1, dy, 0, half), x_up)
 
     def down(dx, dy, half):
-        send(unit(slot(dx, dy), 0, half), unit(slot(dx + 1, dy), 0, half), x_down)
+        send(unit(dx, dy, 0, half), unit(dx + 1, dy, 0, half), x_down)
 
     def across(dx, dy, half):
-        send(unit(slot(dx, dy), 0, half), unit(slot(dx, dy + 1), 0, half), y_mate)
+        send(unit(dx, dy, 0, half), unit(dx, dy + 1, 0, half), y_mate)
 
     def share(dx, dy, half):
-        send(unit(slot(dx, dy), 0, half), unit(slot(dx, dy), 1, half), sibling)
+        send(unit(dx, dy, 0, half), unit(dx, dy, 1, half), sibling)
 
     def take(dx, dy, half):
-        arrived(unit(slot(dx, dy), 0, half))
-
+        arrived(unit(dx, dy, 0, half))
+
+    up(0, 0, 1)
+    down(0, 0, 1)
+    across(0, 0, 1)
+    share(0, 0, 1)
+    squares_0 = condition(g_ref, 0, left, right_parts, mid_ref.at[0], cond_ref.at[0], q_ref)
     across(0, 0, 0)
     up(0, 0, 0)
     down(0, 0, 0)
     share(0, 0, 0)
-    across(0, 0, 1)
-    up(0, 0, 1)
-    down(0, 0, 1)
-    share(0, 0, 1)
-
-    for copy in load_s:
+    squares = jnp.concatenate([squares_0, squares_1], axis=0)
+
+    for copy in load_s + small:
         copy.wait()
     nv_ref[4:5, 0:32] = jnp.sum(squares.T, axis=0, keepdims=True)
 
@@ -231,24 +249,28 @@
         return (x + dx) % 4, (yl + dy) % 2
 
     def multiply(batch):
-        first, last = BATCHES[batch]
-        span = rows(first * 4, 4 * (last - first))
+        first = PLACES.index(BATCHES[batch][0][:2] + (0,) + BATCHES[batch][0][2:])
+        for dx, dy, half in BATCHES[batch]:
+            arrived(unit(dx, dy, 1, half))
+        span = rows(first, 2 * len(BATCHES[batch]))
         p_ref[span, :] = dot(q_ref[span, :], s_ref[...], NT).astype(BF16)
-        for chip in range(first, last):
-            its_x, _ = place(chip)
+        for dx, dy, half in BATCHES[batch]:
+            chip = CHIPS.index((dx, dy))
             for other in range(2):
-                for half in range(2):
-                    u = unit(chip, other, half)
-                    its_core = (core + other) % 2
-                    goal = 4 * (its_x % 2) + 2 * its_core + half
-
-                    @pl.when(goal != z)
-                    def _():
-                        pltpu.make_async_remote_copy(
-                            src_ref=p_ref.at[rows(u)], dst_ref=z_ref.at[chip, (z + 8 - goal) % 8],
-                            send_sem=z_send.at[chip], recv_sem=z_recv.at[chip],
-                            device_id=(ex, yh * 8 + goal), device_id_type=MESH,
-                        ).start()
+                u = unit(dx, dy, other, half)
+                goal = 4 * ((x + dx) % 2) + 2 * ((core + other) % 2) + half
+
+                @pl.when(goal != z)
+                def _():
+                    pltpu.make_async_remote_copy(
+                        src_ref=p_ref.at[rows(u)], dst_ref=z_ref.at[chip, (z + 8 - goal) % 8],
+                        send_sem=z_send.at[chip], recv_sem=z_recv.at[chip],
+                        device_id=(ex, yh * 8 + goal), device_id_type=MESH,
+                    ).start()
+
+                @pl.when(goal == z)
+                def _():
+                    z_ref[chip, 0] = p_ref[rows(u), :]
 
     def mine(chip):
         its_x, _ = place(chip)
@@ -266,98 +288,128 @@
             device_id=(ex, goal * 8 + z), device_id_type=MESH,
         )
 
-    def sum_over_z(batch):
-        first, last = BATCHES[batch]
-        for chip in range(first, last):
-
-            @pl.when(mine(chip))
+    def sum_over_z(dx, dy):
+        chip = CHIPS.index((dx, dy))
+
+        @pl.when(mine(chip))
+        def _():
+            pltpu.make_async_copy(
+                z_ref.at[chip, pl.ds(1, 7)], z_ref.at[chip, pl.ds(1, 7)], z_recv.at[chip]
+            ).wait()
+            total = z_ref[chip, 0].astype(F32)
+            for k in range(1, 8):
+                total = total + z_ref[chip, k].astype(F32)
+            goal = goal_of(chip)
+
+            @pl.when(goal == yh)
             def _():
-                pltpu.make_async_copy(
-                    z_ref.at[chip, pl.ds(1, 7)], z_ref.at[chip, pl.ds(1, 7)], z_recv.at[chip]
-                ).wait()
-                within = (((z % 4) // 2 + core) % 2) * 2 + z % 2
-                start = pl.multiple_of((chip * 4 + within) * UNIT, UNIT)
-                total = p_ref[pl.ds(start, UNIT), :].astype(F32)
-                for k in range(1, 8):
-                    total = total + z_ref[chip, k].astype(F32)
-                goal = goal_of(chip)
-
-                @pl.when(goal == yh)
-                def _():
-                    yr_ref[0] = total
-
-                @pl.when(goal != yh)
-                def _():
-                    ys_ref[chip] = total
-                    y_copy(chip).start()
-
-    arrived(unit(0, 1, 0))
-    arrived(unit(0, 1, 1))
+                yr_ref[0] = total
+
+            @pl.when(goal != yh)
+            def _():
+                ys_ref[chip] = total
+                y_copy(chip).start()
+
     multiply(0)
+
+    take(3, 0, 1)
+    take(1, 0, 1)
+
+    @pl.when(core == 0)
+    def _():
+        up(3, 0, 1)
+        across(1, 0, 1)
+        across(3, 0, 1)
+
+    @pl.when(core == 1)
+    def _():
+        down(1, 0, 1)
+        across(3, 0, 1)
+        across(1, 0, 1)
+
+    share(3, 0, 1)
+    share(1, 0, 1)
+    take(0, 1, 1)
+    share(0, 1, 1)
+    multiply(1)
 
     take(0, 1, 0)
     up(0, 1, 0)
     down(0, 1, 0)
     share(0, 1, 0)
     take(3, 0, 0)
-    up(3, 0, 0)
+    take(1, 0, 0)
+
+    @pl.when(core == 0)
+    def _():
+        down(1, 0, 0)
+
+    @pl.when(core == 1)
+    def _():
+        up(3, 0, 0)
+
     share(3, 0, 0)
-    take(1, 0, 0)
     share(1, 0, 0)
     norms_over_z()
-    take(1, 0, 1)
-    down(1, 0, 1)
-    across(1, 0, 1)
-    share(1, 0, 1)
-    take(3, 0, 1)
-    across(3, 0, 1)
-    share(3, 0, 1)
-    take(0, 1, 1)
-    share(0, 1, 1)
-    for chip in range(*BATCHES[1]):
-        arrived(unit(chip, 1, 0))
-        arrived(unit(chip, 1, 1))
-    multiply(1)
-    sum_over_z(0)
-
+    sum_over_z(0, 0)
+    multiply(2)
+
+    take(2, 0, 1)
+    share(2, 0, 1)
+
+    @pl.when(core == 0)
+    def _():
+        take(1, 1, 1)
+        down(1, 1, 1)
+        share(1, 1, 1)
+
+    @pl.when(core == 1)
+    def _():
+        take(3, 1, 1)
+        up(3, 1, 1)
+        share(3, 1, 1)
+
+    take(3, 1, 0)
+    take(1, 1, 0)
+
+    @pl.when(core == 0)
+    def _():
+        up(3, 1, 0)
+
+    @pl.when(core == 1)
+    def _():
+        down(1, 1, 0)
+
+    share(3, 1, 0)
+    share(1, 1, 0)
+    multiply(3)
     take(2, 0, 0)
     share(2, 0, 0)
-    take(2, 0, 1)
-    across(2, 0, 1)
-    share(2, 0, 1)
-    take(3, 1, 0)
 
     @pl.when(core == 0)
     def _():
-        up(3, 1, 0)
-
-    share(3, 1, 0)
-    take(1, 1, 0)
+        take(3, 1, 1)
+        share(3, 1, 1)
 
     @pl.when(core == 1)
     def _():
-        down(1, 1, 0)
-
-    share(1, 1, 0)
+        take(1, 1, 1)
+        share(1, 1, 1)
+
     norms_over_y()
-    take(1, 1, 1)
-    share(1, 1, 1)
-    take(3, 1, 1)
-    share(3, 1, 1)
-    for chip in range(*BATCHES[2]):
-        arrived(unit(chip, 1, 0))
-        arrived(unit(chip, 1, 1))
-    multiply(2)
-    sum_over_z(1)
+    sum_over_z(0, 1)
+    sum_over_z(1, 0)
+    sum_over_z(3, 0)
+    multiply(4)
 
     take(2, 1, 0)
     share(2, 1, 0)
     take(2, 1, 1)
     share(2, 1, 1)
-    arrived(unit(7, 1, 0))
-    arrived(unit(7, 1, 1))
-    multiply(3)
-    sum_over_z(2)
+    multiply(5)
+    sum_over_z(2, 0)
+    sum_over_z(1, 1)
+    sum_over_z(3, 1)
 
     @pl.when(ex == owner)
     def _():
@@ -378,7 +430,7 @@
         for k in range(15):
             b_norm(k).wait_send()
 
-    sum_over_z(3)
+    sum_over_z(2, 1)
     for chip in range(8):
 
         @pl.when(mine(chip))
@@ -417,19 +469,21 @@
     count, _, width = query_grads.shape
     examples = store.shape[0]
     vmem = pl.BlockSpec(memory_space=pltpu.VMEM)
-    smem = pl.BlockSpec(memory_space=pltpu.SMEM)
-    hbm = pl.BlockSpec(memory_space=pl.ANY)
+    hbm = pl.BlockSpec(memory_space=pltpu.HBM)
     dma = pltpu.SemaphoreType.DMA
     return pl.pallas_call(
         kernel,
         out_shape=jax.ShapeDtypeStruct((UNIT, examples), F32),
-        in_specs=[hbm, hbm, vmem, vmem, smem, smem],
+        in_specs=[hbm] * 5 + [pl.BlockSpec(memory_space=pltpu.SMEM)],
         out_specs=vmem,
         scratch_shapes=[
             pltpu.VMEM((count, width), BF16),
             pltpu.VMEM((examples, width), BF16),
-            pltpu.VMEM((2, 1024, 128), F32),
-            pltpu.VMEM((1024, 128), F32),
+            pltpu.VMEM((SIDE, SIDE), F32),
+            pltpu.VMEM((SIDE, SIDE), F32),
+            pltpu.SMEM(query_ids.shape, jnp.int32),
+            pltpu.VMEM((2, 2, 512, 128), F32),
+            pltpu.VMEM((2, 512, 128), F32),
             pltpu.VMEM((512, width), BF16),
             pltpu.VMEM((512, examples), BF16),
             pltpu.VMEM((8, 8, UNIT, examples), BF16),
@@ -440,7 +494,7 @@
             pltpu.VMEM((4, 8, 128), F32),
             pltpu.VMEM((8, 128), F32),
             pltpu.VMEM((8, 128), F32),
-            dma((5,)),
+            dma((8,)),
             dma((1,)),
             dma((32,)),
             dma((8,)),
@@ -455,7 +509,7 @@
             dma((1,)),
         ],
         compiler_params=pltpu.CompilerParams(
-            collective_id=0, has_side_effects=True, vmem_limit_bytes=40 * 2**20
+            collective_id=0, has_side_effects=True, vmem_limit_bytes=60 * 2**20
         ),
         cost_estimate=pl.CostEstimate(
             flops=2 * 512 * examples * width, bytes_accessed=(examples + count) * width * 2, transcendentals=0

time: 54.4 us -> 50.1 us (0.921)
  the two profiles are of different devices: /device:TPU:24 before, /device:TPU:12 now
where the time goes in v2:
time: 50.1 us; the launch traced here: 49.9 us
  Pallas kernels  47.9 us (96%)
  local copies, waits for them, and re-layouts  1.38 us (3%)
  between operations  0.66 us (1%)
    pallas_call x1, Pallas kernels, per_device(): pl.pallas_call(kernel, out_shape=jax.ShapeDtypeStruct((UNIT, examples), F...  47.9 us
    unnamed x1, local copies, waits for them, and re-layouts  1.38 us

profile of v2, /device:TPU:12, one launch (start us, length us, event | category | flops | bytes accessed | tf_op | source)
XLA Modules:
  0.0 49.9 jit_solution(14660699953022450455)
XLA Ops:
  0.7 47.9 %shard_map.64 = f32[16,512]{1,0:T(8,128)} custom-call(bf16[32,4096]{1,0:T(8,128)(2,1)} %bitcast.5, bf16[512,4096]{1,0:T(8,128)(2,1)} %bitcast.4, f32[64,64]{1,0:T(8,128)} %bitcast.6, f32[64,64]{1,0:T(8,128)} %bitcast.7, s32[512]{0:T(512)} %ids_hbm.1, s32[1]{0:T(128)S(6)} %copy.8.off_ref), custom_call_target="tpu_custom_call" | custom-call | flops 2147483648 | bytes 4456448 | tf_op jit(solution)/shard_map/pallas_call | solution.py:474
  48.5 1.4 %copy.9 = f32[16,512]{1,0:T(8,128)} copy(f32[16,512]{1,0:T(8,128)} %shard_map.64) | data formatting | bytes 65536

commit v3 on v2

--- a/solution.py
+++ b/solution.py
@@ -15,10 +15,8 @@
 CHIPS = [(0, 0), (0, 1), (1, 0), (3, 0), (2, 0), (1, 1), (3, 1), (2, 1)]
 BATCHES = [
     [(0, 0, 0), (0, 0, 1)],
-    [(1, 0, 1), (3, 0, 1), (0, 1, 1)],
-    [(1, 0, 0), (3, 0, 0), (0, 1, 0)],
-    [(2, 0, 1), (1, 1, 0), (3, 1, 0)],
-    [(2, 0, 0), (1, 1, 1), (3, 1, 1)],
+    [(1, 0, 1), (3, 0, 1), (0, 1, 1), (1, 0, 0), (3, 0, 0), (0, 1, 0)],
+    [(2, 0, 1), (1, 1, 0), (3, 1, 0), (2, 0, 0), (1, 1, 1), (3, 1, 1)],
     [(2, 1, 0), (2, 1, 1)],
 ]
 PLACES = [
@@ -121,6 +119,14 @@
     x_up = yl * 8 + ((x + 1) % 4) * 2 + core
     x_down = yl * 8 + ((x + 3) % 4) * 2 + core
     y_mate = (ex + 8) % 16
+    examples = s_ref.shape[0]
+
+    first = [
+        pltpu.make_async_copy(src, dst, load_sem.at[4 + i])
+        for i, (src, dst) in enumerate([(right_hbm, right_ref), (g_hbm, g_ref), (left_hbm, left_ref)])
+    ]
+    for copy in first:
+        copy.start()
 
     barrier = pltpu.get_barrier_semaphore()
     for k in range(1, 16):
@@ -130,13 +136,7 @@
     for k in range(1, 4):
         pl.semaphore_signal(barrier, inc=1, device_id=(ex, (lay + 8 * k) % 32), device_id_type=MESH)
 
-    first = [
-        pltpu.make_async_copy(src, dst, load_sem.at[4 + i])
-        for i, (src, dst) in enumerate([(right_hbm, right_ref), (g_hbm, g_ref), (left_hbm, left_ref)])
-    ]
     small = [pltpu.make_async_copy(ids_hbm, ids_ref, load_sem.at[7])]
-    for copy in first:
-        copy.start()
     load_s = [
         pltpu.make_async_copy(s_hbm.at[pl.ds(128 * i, 128)], s_ref.at[pl.ds(128 * i, 128)], load_sem.at[i])
         for i in range(4)
@@ -151,26 +151,29 @@
 
     pl.semaphore_wait(barrier, 25)
 
-    def send(src, dst, to):
+    width = q_ref.shape[1]
+
+    def send(src, dst, to, part):
+        span = pl.ds(0, width) if part is None else pl.ds(part * (width // 2), width // 2)
         pltpu.make_async_remote_copy(
-            src_ref=q_ref.at[rows(src)], dst_ref=q_ref.at[rows(dst)], send_sem=g_send.at[0],
+            src_ref=q_ref.at[rows(src), span], dst_ref=q_ref.at[rows(dst), span], send_sem=g_send.at[0],
             recv_sem=g_recv.at[dst], device_id=(to, lay), device_id_type=MESH,
         ).start()
 
     def arrived(u):
         pltpu.make_async_copy(q_ref.at[rows(u)], q_ref.at[rows(u)], g_recv.at[u]).wait()
 
-    def up(dx, dy, half):
-        send(unit(dx, dy, 0, half), unit(dx - 1, dy, 0, half), x_up)
-
-    def down(dx, dy, half):
-        send(unit(dx, dy, 0, half), unit(dx + 1, dy, 0, half), x_down)
-
-    def across(dx, dy, half):
-        send(unit(dx, dy, 0, half), unit(dx, dy + 1, 0, half), y_mate)
-
-    def share(dx, dy, half):
-        send(unit(dx, dy, 0, half), unit(dx, dy, 1, half), sibling)
+    def up(dx, dy, half, part=None):
+        send(unit(dx, dy, 0, half), unit(dx - 1, dy, 0, half), x_up, part)
+
+    def down(dx, dy, half, part=None):
+        send(unit(dx, dy, 0, half), unit(dx + 1, dy, 0, half), x_down, part)
+
+    def across(dx, dy, half, part=None):
+        send(unit(dx, dy, 0, half), unit(dx, dy + 1, 0, half), y_mate, part)
+
+    def share(dx, dy, half, part=None):
+        send(unit(dx, dy, 0, half), unit(dx, dy, 1, half), sibling, part)
 
     def take(dx, dy, half):
         arrived(unit(dx, dy, 0, half))
@@ -248,29 +251,33 @@
         dx, dy = CHIPS[chip]
         return (x + dx) % 4, (yl + dy) % 2
 
-    def multiply(batch):
+    def multiply(batch, cuts=1):
         first = PLACES.index(BATCHES[batch][0][:2] + (0,) + BATCHES[batch][0][2:])
         for dx, dy, half in BATCHES[batch]:
             arrived(unit(dx, dy, 1, half))
         span = rows(first, 2 * len(BATCHES[batch]))
-        p_ref[span, :] = dot(q_ref[span, :], s_ref[...], NT).astype(BF16)
-        for dx, dy, half in BATCHES[batch]:
-            chip = CHIPS.index((dx, dy))
-            for other in range(2):
-                u = unit(dx, dy, other, half)
-                goal = 4 * ((x + dx) % 2) + 2 * ((core + other) % 2) + half
-
-                @pl.when(goal != z)
-                def _():
-                    pltpu.make_async_remote_copy(
-                        src_ref=p_ref.at[rows(u)], dst_ref=z_ref.at[chip, (z + 8 - goal) % 8],
-                        send_sem=z_send.at[chip], recv_sem=z_recv.at[chip],
-                        device_id=(ex, yh * 8 + goal), device_id_type=MESH,
-                    ).start()
-
-                @pl.when(goal == z)
-                def _():
-                    z_ref[chip, 0] = p_ref[rows(u), :]
+        wide = examples // cuts
+        for cut in range(cuts):
+            columns = slice(cut * wide, (cut + 1) * wide)
+            p_ref[span, columns] = dot(q_ref[span, :], s_ref[columns, :], NT).astype(BF16)
+            for dx, dy, half in BATCHES[batch]:
+                chip = CHIPS.index((dx, dy))
+                for other in range(2):
+                    u = unit(dx, dy, other, half)
+                    goal = 4 * ((x + dx) % 2) + 2 * ((core + other) % 2) + half
+
+                    @pl.when(goal != z)
+                    def _():
+                        pltpu.make_async_remote_copy(
+                            src_ref=p_ref.at[rows(u), pl.ds(cut * wide, wide)],
+                            dst_ref=z_ref.at[chip, (z + 8 - goal) % 8, :, pl.ds(cut * wide, wide)],
+                            send_sem=z_send.at[chip], recv_sem=z_recv.at[chip],
+                            device_id=(ex, yh * 8 + goal), device_id_type=MESH,
+                        ).start()
+
+                    @pl.when(goal == z)
+                    def _():
+                        z_ref[chip, 0, :, columns] = p_ref[rows(u), columns]
 
     def mine(chip):
         its_x, _ = place(chip)
@@ -331,7 +338,6 @@
     share(1, 0, 1)
     take(0, 1, 1)
     share(0, 1, 1)
-    multiply(1)
 
     take(0, 1, 0)
     up(0, 1, 0)
@@ -351,22 +357,23 @@
     share(3, 0, 0)
     share(1, 0, 0)
     norms_over_z()
+    multiply(1)
     sum_over_z(0, 0)
-    multiply(2)
 
     take(2, 0, 1)
+    across(2, 0, 1, 1)
     share(2, 0, 1)
 
     @pl.when(core == 0)
     def _():
         take(1, 1, 1)
-        down(1, 1, 1)
+        down(1, 1, 1, 0)
         share(1, 1, 1)
 
     @pl.when(core == 1)
     def _():
         take(3, 1, 1)
-        up(3, 1, 1)
+        up(3, 1, 1, 0)
         share(3, 1, 1)
 
     take(3, 1, 0)
@@ -382,7 +389,6 @@
 
     share(3, 1, 0)
     share(1, 1, 0)
-    multiply(3)
     take(2, 0, 0)
     share(2, 0, 0)
 
@@ -397,16 +403,16 @@
         share(1, 1, 1)
 
     norms_over_y()
+
+    take(2, 1, 0)
+    share(2, 1, 0)
+    multiply(2)
+    take(2, 1, 1)
+    share(2, 1, 1)
     sum_over_z(0, 1)
     sum_over_z(1, 0)
     sum_over_z(3, 0)
-    multiply(4)
-
-    take(2, 1, 0)
-    share(2, 1, 0)
-    take(2, 1, 1)
-    share(2, 1, 1)
-    multiply(5)
+    multiply(3, cuts=2)
     sum_over_z(2, 0)
     sum_over_z(1, 1)
     sum_over_z(3, 1)
@@ -473,7 +479,7 @@
     dma = pltpu.SemaphoreType.DMA
     return pl.pallas_call(
         kernel,
-        out_shape=jax.ShapeDtypeStruct((UNIT, examples), F32),
+        out_shape=pltpu.VMEM((UNIT, examples), F32),
         in_specs=[hbm] * 5 + [pl.BlockSpec(memory_space=pltpu.SMEM)],
         out_specs=vmem,
         scratch_shapes=[

time: 50.1 us -> 46.8 us (0.934)
  the two profiles are of different devices: /device:TPU:12 before, /device:TPU:24 now
where the time goes in v3:
time: 46.8 us; the launch traced here: 46.7 us
  Pallas kernels  45.4 us (97%)
  between operations  0.66 us (1%)
  local copies, waits for them, and re-layouts  0.62 us (1%)
    pallas_call x1, Pallas kernels, per_device(): pl.pallas_call(kernel, out_shape=pltpu.VMEM((UNIT, examples), F32), in_sp...  45.4 us

profile of v3, /device:TPU:24, one launch (start us, length us, event | category | flops | bytes accessed | tf_op | source)
XLA Modules:
  0.0 46.7 jit_solution(6111706016714607175)
XLA Ops:
  0.7 45.4 %shard_map.64 = f32[16,512]{1,0:T(8,128)S(1)} custom-call(bf16[32,4096]{1,0:T(8,128)(2,1)} %bitcast.5, bf16[512,4096]{1,0:T(8,128)(2,1)} %bitcast.4, f32[64,64]{1,0:T(8,128)} %bitcast.6, f32[64,64]{1,0:T(8,128)} %bitcast.7, s32[512]{0:T(512)} %ids_hbm.1, s32[1]{0:T(128)S(6)} %copy.9.off_ref), custom_call_target="tpu_custom_call" | custom-call | flops 2147483648 | bytes 4456448 | tf_op jit(solution)/shard_map/pallas_call | solution.py:480
  46.1 0.6 %copy.8 = f32[16,512]{1,0:T(8,128)} copy(f32[16,512]{1,0:T(8,128)S(1)} %shard_map.64) | data formatting | bytes 65536

commit v4 on v3

--- a/solution.py
+++ b/solution.py
@@ -144,9 +144,10 @@
     for copy in load_s + small:
         copy.start()
     nv_ref[...] = jnp.zeros_like(nv_ref)
-    for copy in first:
-        copy.wait()
+    first[0].wait()
+    first[2].wait()
     left, right_parts = factors(left_ref, right_ref, cond_ref.at[1])
+    first[1].wait()
     squares_1 = condition(g_ref, 1, left, right_parts, mid_ref.at[1], cond_ref.at[1], q_ref)
 
     pl.semaphore_wait(barrier, 25)
@@ -412,7 +413,7 @@
     sum_over_z(0, 1)
     sum_over_z(1, 0)
     sum_over_z(3, 0)
-    multiply(3, cuts=2)
+    multiply(3)
     sum_over_z(2, 0)
     sum_over_z(1, 1)
     sum_over_z(3, 1)

time: 46.8 us -> 46.5 us (level)
  no operation moved by 1% of the time
where the time goes in v4:
time: 46.5 us; the launch traced here: 46.4 us
  Pallas kernels  45.1 us (97%)
  between operations  0.66 us (1%)
  local copies, waits for them, and re-layouts  0.62 us (1%)
    pallas_call x1, Pallas kernels, per_device(): pl.pallas_call(kernel, out_shape=pltpu.VMEM((UNIT, examples), F32), in_sp...  45.1 us

profile of v4, /device:TPU:24, one launch (start us, length us, event | category | flops | bytes accessed | tf_op | source)
XLA Modules:
  0.0 46.4 jit_solution(5109862545754345826)
XLA Ops:
  0.7 45.1 %shard_map.64 = f32[16,512]{1,0:T(8,128)S(1)} custom-call(bf16[32,4096]{1,0:T(8,128)(2,1)} %bitcast.5, bf16[512,4096]{1,0:T(8,128)(2,1)} %bitcast.4, f32[64,64]{1,0:T(8,128)} %bitcast.6, f32[64,64]{1,0:T(8,128)} %bitcast.7, s32[512]{0:T(512)} %ids_hbm.1, s32[1]{0:T(128)S(6)} %copy.9.off_ref), custom_call_target="tpu_custom_call" | custom-call | flops 2147483648 | bytes 4456448 | tf_op jit(solution)/shard_map/pallas_call | solution.py:481
  45.8 0.6 %copy.8 = f32[16,512]{1,0:T(8,128)} copy(f32[16,512]{1,0:T(8,128)S(1)} %shard_map.64) | data formatting | bytes 65536

commit v5 on v4

--- a/solution.py
+++ b/solution.py
@@ -344,19 +344,22 @@
     up(0, 1, 0)
     down(0, 1, 0)
     share(0, 1, 0)
-    take(3, 0, 0)
-    take(1, 0, 0)
-
     @pl.when(core == 0)
     def _():
+        take(1, 0, 0)
         down(1, 0, 0)
+        share(1, 0, 0)
+        take(3, 0, 0)
+        share(3, 0, 0)
 
     @pl.when(core == 1)
     def _():
+        take(3, 0, 0)
         up(3, 0, 0)
-
-    share(3, 0, 0)
-    share(1, 0, 0)
+        share(3, 0, 0)
+        take(1, 0, 0)
+        share(1, 0, 0)
+
     norms_over_z()
     multiply(1)
     sum_over_z(0, 0)
@@ -377,19 +380,22 @@
         up(3, 1, 1, 0)
         share(3, 1, 1)
 
-    take(3, 1, 0)
-    take(1, 1, 0)
-
     @pl.when(core == 0)
     def _():
+        take(3, 1, 0)
         up(3, 1, 0)
+        share(3, 1, 0)
+        take(1, 1, 0)
+        share(1, 1, 0)
 
     @pl.when(core == 1)
     def _():
+        take(1, 1, 0)
         down(1, 1, 0)
-
-    share(3, 1, 0)
-    share(1, 1, 0)
+        share(1, 1, 0)
+        take(3, 1, 0)
+        share(3, 1, 0)
+
     take(2, 0, 0)
     share(2, 0, 0)
 

time: 46.5 us -> 46.5 us (level)
  no operation moved by 1% of the time
where the time goes in v5:
time: 46.5 us; the launch traced here: 46.4 us
  Pallas kernels  45.1 us (97%)
  between operations  0.66 us (1%)
  local copies, waits for them, and re-layouts  0.62 us (1%)
    pallas_call x1, Pallas kernels, per_device(): pl.pallas_call(kernel, out_shape=pltpu.VMEM((UNIT, examples), F32), in_sp...  45.1 us

profile of v5, /device:TPU:24, one launch (start us, length us, event | category | flops | bytes accessed | tf_op | source)
XLA Modules:
  0.0 46.4 jit_solution(16650948046677734615)
XLA Ops:
  0.7 45.1 %shard_map.64 = f32[16,512]{1,0:T(8,128)S(1)} custom-call(bf16[32,4096]{1,0:T(8,128)(2,1)} %bitcast.5, bf16[512,4096]{1,0:T(8,128)(2,1)} %bitcast.4, f32[64,64]{1,0:T(8,128)} %bitcast.6, f32[64,64]{1,0:T(8,128)} %bitcast.7, s32[512]{0:T(512)} %ids_hbm.1, s32[1]{0:T(128)S(6)} %copy.9.off_ref), custom_call_target="tpu_custom_call" | custom-call | flops 2147483648 | bytes 4456448 | tf_op jit(solution)/shard_map/pallas_call | solution.py:487
  45.8 0.6 %copy.8 = f32[16,512]{1,0:T(8,128)} copy(f32[16,512]{1,0:T(8,128)S(1)} %shard_map.64) | data formatting | bytes 65536
